TPU v7x, 128 devices: a whole 4x4x4 slice. The times are simulated.
128 devices in a mesh: row: 8 (over y, x_hi), col: 16 (over z, x_lo, core).
Axes of the slice: x: 4 (x_hi: 2, x_lo: 2; x = x_hi * 2 + x_lo), y: 4, z: 4, core: 2. Of those that a mesh axis runs over, the one named last changes fastest.
Arguments:
- teacher: bfloat16 [16384, 256], replicated, may hold values from -4 to 4
- panel_ids: int32 [2048], P('col'), may hold values from 0 to 16383
- rest_ids: int32 [8, 16, 128], P('row', 'col'), may hold values from 0 to 16383
- inverse: bfloat16 [2048, 2048], replicated, may hold values from -1 to 1, as said below
Outputs:
- trailing: float32 [16, 8, 128, 8, 16, 128], P(None, 'row', None, None, 'col')
- panel_rows: bfloat16 [8, 16, 128, 2048], P('row', 'col')
Inputs may be any that keep to these rules, and one draw needn't show every extreme that they name: `inverse`: zero above the diagonal.
All inputs are finite; a program needn't handle non-finite values.
Results may differ from a plain program's by a relative error of at most 0.0049.
Values may be sent and summed in bfloat16 or wider, within the bound.
No kernel may reach another device: no remote copies, remote signals or barrier semaphores. Data moves between devices by JAX's collectives and lax.ppermute only.
A program may use at most 128 MiB of HBM per device.

v0:
```python
import jax
import jax.numpy as jnp
from jax import lax
from jax.sharding import PartitionSpec as P


def gaussian(left_rows, right_rows, inv_scale):
    sq_left = jnp.sum(jnp.square(left_rows.astype(jnp.float32)), axis=-1)
    sq_right = jnp.sum(jnp.square(right_rows.astype(jnp.float32)), axis=-1)
    inner = lax.dot_general(
        left_rows, right_rows, (((1,), (1,)), ((), ())), preferred_element_type=jnp.float32
    )
    return jnp.exp(-inv_scale * (sq_left[:, None] + sq_right[None, :] - 2.0 * inner))


def factor(rows_emb, panel_emb, inverse, inv_scale):
    kernel = gaussian(rows_emb, panel_emb, inv_scale).astype(jnp.bfloat16)
    block_width = inverse.shape[0] // 4
    pieces = []
    for block_at in range(4):
        finish = (block_at + 1) * block_width
        pieces.append(
            lax.dot_general(
                kernel[:, :finish],
                inverse[block_at * block_width : finish, :finish],
                (((1,), (1,)), ((), ())),
                preferred_element_type=jnp.float32,
            )
        )
    return jnp.concatenate(pieces, 1).astype(jnp.bfloat16)


def shards(teacher, panel_ids, rest_ids, inverse):
    n_row = lax.axis_size("row")
    n_col = lax.axis_size("col")
    row_at = lax.axis_index("row")
    col_at = lax.axis_index("col")
    stretch_rows = rest_ids.shape[2]
    inv_scale = 2.0 / teacher.shape[1]
    gathered = lax.all_gather(rest_ids, ("row", "col"), axis=0, tiled=True)
    blocks = gathered.reshape(n_row * n_col, stretch_rows)
    panel = lax.all_gather(panel_ids, "col", axis=0, tiled=True)
    panel_emb = teacher[panel]
    own_ids = lax.dynamic_slice_in_dim(blocks, row_at * n_col + col_at, 1, 0).reshape(stretch_rows)
    col_ids = lax.dynamic_slice_in_dim(
        blocks.reshape(n_row, n_col, stretch_rows), col_at, 1, 1
    ).reshape(-1)
    row_ids = lax.dynamic_slice_in_dim(
        blocks.reshape(n_col, n_row, stretch_rows), row_at, 1, 1
    ).reshape(-1)
    own_factor = factor(teacher[own_ids], panel_emb, inverse, inv_scale)
    col_emb = teacher[col_ids]
    col_factor = lax.all_gather(own_factor, "row", axis=0, tiled=True)
    row_emb = teacher[row_ids]
    kernel = gaussian(row_emb, col_emb, inv_scale)
    local_ids = lax.dynamic_slice_in_dim(blocks, col_at * n_row + row_at, 1, 0).reshape(
        stretch_rows
    )
    local_factor = factor(teacher[local_ids], panel_emb, inverse, inv_scale)
    update = lax.dot_general(
        lax.all_gather(local_factor, "col", axis=0, tiled=True),
        col_factor,
        (((1,), (1,)), ((), ())),
        preferred_element_type=jnp.float32,
    )
    rows_local = jnp.arange(n_col * stretch_rows, dtype=jnp.int32)
    row_index = (
        rows_local // stretch_rows * n_row + row_at
    ) * stretch_rows + rows_local % stretch_rows
    cols_local = jnp.arange(n_row * stretch_rows, dtype=jnp.int32)
    col_index = (
        cols_local // stretch_rows * n_col + col_at
    ) * stretch_rows + cols_local % stretch_rows
    result = kernel - update
    trailing = jnp.where(row_index[:, None] >= col_index[None, :], result, jnp.zeros_like(result))
    return (
        trailing.reshape(n_col, 1, stretch_rows, n_row, 1, stretch_rows),
        own_factor.reshape(1, 1, stretch_rows, own_factor.shape[1]),
    )


def solution(mesh):
    return jax.shard_map(
        shards,
        mesh=mesh,
        in_specs=(P(), P("col"), P("row", "col", None), P()),
        out_specs=(P(None, "row", None, None, "col", None), P("row", "col", None, None)),
        check_vma=False,
    )
```

profile of v0, /device:TPU:1, one launch (start us, length us, event | category | flops | bytes accessed | tf_op | source)
XLA Modules:
  0.0 375.2 jit_solution(5608160516560032385)
XLA Ops:
  7.2 179.5 %all_gather.12 = s32[128,1,128]{2,1,0:T(1,128)S(1)} all-gather(s32[1,1,128]{2,1,0:T(1,128)} %param.6), channel_id=1, replica_groups=mesh['row'=8,'col'=16] {'row','col'}, dimensions={0}, use_global_device_ids=true | all-gather | bytes 66048 | tf_op jit(solution)/shard_map/all_gather | solution.py:40
  186.8 5.2 %gather_fusion.4 = bf16[128,256]{1,0:T(8,128)(2,1)S(1)} fusion(bf16[16384,256]{1,0:T(8,128)(2,1)} %param.4, s32[1024]{0:T(1024)S(1)} %get-tuple-element.8), kind=kCustom, calls=%fused_computation.4 | custom fusion | bytes 131584 | tf_op jit(solution)/shard_map/gather | solution.py:51
  192.1 16.3 %all-gather = s32[16,1,128]{2,1,0:T(1,128)S(1)} all-gather(s32[1,1,128]{2,1,0:T(1,128)} %bitcast.57), channel_id=1, replica_groups=mesh['row'=8,'col'=16] {'col'}, dimensions={0}, use_global_device_ids=true | all-gather | bytes 8704 | tf_op jit(solution)/shard_map/all_gather | solution.py:42
  208.4 11.1 %gather_fusion.3 = bf16[2048,256]{1,0:T(8,128)(2,1)S(1)} fusion(bf16[16384,256]{1,0:T(8,128)(2,1)} %param.4, s32[2048]{0:T(1024)S(1)} %fusion.49), kind=kCustom, calls=%fused_computation.3 | custom fusion | bytes 2105344 | tf_op jit(solution)/shard_map/gather | solution.py:43
  220.4 1.4 convolution_convert_fusion
  221.7 1.7 convolution_convert_fusion.2
  223.5 2.4 fusion.19
  225.9 2.1 fusion.25
  228.0 0.9 pad_maximum_fusion.1
  228.9 5.2 %gather_fusion.2 = bf16[128,256]{1,0:T(8,128)(2,1)S(1)} fusion(bf16[16384,256]{1,0:T(8,128)(2,1)} %param.4, s32[1024]{0:T(1024)S(1)} %get-tuple-element.9), kind=kCustom, calls=%fused_computation.2 | custom fusion | bytes 131584 | tf_op jit(solution)/shard_map/gather | solution.py:59
  234.2 0.5 fusion.6
  234.8 1.4 convolution_convert_fusion.1
  236.1 1.7 convolution_convert_fusion.3
  237.9 2.1 fusion.22
  239.9 2.4 fusion.16
  242.4 0.8 pad_maximum_fusion
  243.3 11.3 %gather_fusion = bf16[2048,256]{1,0:T(8,128)(2,1)S(1)} fusion(bf16[16384,256]{1,0:T(8,128)(2,1)} %param.4, s32[2048]{0:T(1024)S(1)} %broadcast_clamp_fusion), kind=kCustom, calls=%fused_computation | custom fusion | bytes 2105344 | tf_op jit(solution)/shard_map/gather | solution.py:54
  254.7 7.9 %gather_fusion.1 = bf16[1024,256]{1,0:T(8,128)(2,1)S(1)} fusion(bf16[16384,256]{1,0:T(8,128)(2,1)} %param.4, s32[1024]{0:T(1024)S(1)} %broadcast_clamp_fusion.1), kind=kCustom, calls=%fused_computation.1 | custom fusion | bytes 1052672 | tf_op jit(solution)/shard_map/gather | solution.py:52
  263.2 0.8 pad_maximum_fusion.2
  264.0 30.3 %all-gather.6.cloned.1.call-done = bf16[1024,2048]{1,0:T(8,128)(2,1)} async-done(((bf16[128,2048]{1,0:T(8,128)(2,1)}), bf16[1024,2048]{1,0:T(8,128)(2,1)}) %all-gather.6.cloned.1.call-update) | async-done | bytes 4194320 | tf_op jit(solution)/shard_map/all_gather | solution.py:53
  294.4 53.2 %all-gather.4.cloned.1.call-done = bf16[2048,2048]{1,0:T(8,128)(2,1)} async-done(((bf16[128,2048]{1,0:T(8,128)(2,1)}), bf16[2048,2048]{1,0:T(8,128)(2,1)}) %all-gather.4.cloned.1.call-update) | async-done | bytes 8388624 | tf_op jit(solution)/shard_map/all_gather | solution.py:61
  347.6 12.5 %fusion.65 = f32[2048,1024]{1,0:T(8,128)S(1)} fusion(bf16[2048,2048]{1,0:T(8,128)(2,1)} %all-gather.4.cloned.1.call-done, bf16[1024,2048]{1,0:T(8,128)(2,1)} %all-gather.6.cloned.1.call-done), kind=kOutput, calls=%fused_computation.96 | convolution fusion | flops 8589934592 | bytes 20971520 | tf_op jit(solution)/shard_map/dot_general | solution.py:60
  360.1 2.8 select_bitcast_fusion
  362.9 5.5 %copy.8 = f32[256,8,8,128]{3,2,1,0:T(8,128)} copy(f32[256,8,8,128]{3,1,2,0:T(8,128)S(1)} %select_bitcast_fusion) | data formatting | bytes 16777216
  (19 shorter events, 1.8 us)
Async XLA Ops:
  7.2 287.2 %all-gather.6.cloned.1.call-start = ((), (), s32[]{:S(2)}) async-start(), calls=%async_computation.1 | async-start | bytes 4718592 | tf_op jit(solution)/shard_map/all_gather | solution.py:53
  228.9 118.7 %all-gather.4.cloned.1.call-start = ((), (), s32[]{:S(2)}) async-start(), calls=%async_computation | async-start | bytes 8912896 | tf_op jit(solution)/shard_map/all_gather | solution.py:61
Sparse Core Ops, SparseCore 0:
  229.0 65.3 all-gather.5
  296.6 50.8 all-gather.3
where the time goes:
time: 376 us; the launch traced here: 375 us
  blocking collectives  196 us (52%)
  waiting for transfers between devices  83.6 us (22%)
  local copies, waits for them, and re-layouts  46.3 us (12%)
  matrix products  31.4 us (8%)
  between operations  14.2 us (4%)
  other arithmetic  3.77 us (1%)
    all_gather x1, blocking collectives, shards(): gathered = lax.all_gather(rest_ids, ('row', 'col'), axis=0, tiled=True)  180 us
    all_gather x1, waiting for transfers between devices, shards(): lax.all_gather(local_factor, 'col', axis=0, tiled=True)  53.2 us
    all_gather x1, waiting for transfers between devices, shards(): col_factor = lax.all_gather(own_factor, 'row', axis=0, tiled=True)  30.3 us
    all_gather x1, blocking collectives, shards(): panel = lax.all_gather(panel_ids, 'col', axis=0, tiled=True)  16.3 us
    dot_general x8, matrix products, factor(): lax.dot_general(kernel[:, :finish], inverse[block_at * block_width:finish...  15.1 us
    dot_general x1, matrix products, shards(): lax.dot_general(lax.all_gather(local_factor, 'col', axis=0, tiled=True),...  12.5 us
    gather x1, local copies, waits for them, and re-layouts, shards(): row_emb = teacher[row_ids]  11.3 us
    gather x1, local copies, waits for them, and re-layouts, shards(): panel_emb = teacher[panel]  11.1 us
  transfers between devices with their start and end apart: 2, of which 2 were waited for; matrix products, arithmetic and copies ran while one was open for 9% of the time, Pallas kernels for 0%

commit v1 on v0

--- a/solution.py
+++ b/solution.py
@@ -37,7 +37,10 @@
     col_at = lax.axis_index("col")
     stretch_rows = rest_ids.shape[2]
     inv_scale = 2.0 / teacher.shape[1]
-    gathered = lax.all_gather(rest_ids, ("row", "col"), axis=0, tiled=True)
+    gathered = jnp.concatenate(
+        lax.all_to_all(jnp.stack([rest_ids] * lax.axis_size(("row", "col"))), ("row", "col"), 0, 0),
+        axis=0,
+    )
     blocks = gathered.reshape(n_row * n_col, stretch_rows)
     panel = lax.all_gather(panel_ids, "col", axis=0, tiled=True)
     panel_emb = teacher[panel]

time: 376 us -> 217 us (0.58)
  blocking collectives: 196 us -> 20.6 us
  starting transfers between devices: 0.08 us -> 11.6 us
    all_gather x1 -> x0, blocking collectives: 180 us -> none  [shards(): gathered = lax.all_gather(rest_ids, ('row', 'col'), axis=0, tiled=True)]
    all_to_all x0 -> x1, starting transfers between devices: none -> 11.5 us  [shards(): lax.all_to_all(jnp.stack([rest_ids] * lax.axis_size(('row', 'col'))), ('r...]
    all_gather x1, blocking collectives: 16.3 us -> 20.6 us  [shards(): panel = lax.all_gather(panel_ids, 'col', axis=0, tiled=True)]
  transfers between devices with their start and end apart: 2 -> 3, of which waited for: 2 -> 2; matrix products, arithmetic and copies ran while one was open for 9% -> 22% of each run, Pallas kernels for 0% -> 0%
where the time goes in v1:
time: 217 us; the launch traced here: 216 us
  waiting for transfers between devices  87 us (40%)
  local copies, waits for them, and re-layouts  47.6 us (22%)
  matrix products  31.6 us (15%)
  blocking collectives  20.6 us (9%)
  between operations  14.3 us (7%)
  starting transfers between devices  11.6 us (5%)
  other arithmetic  3.77 us (2%)
    all_gather x1, waiting for transfers between devices, shards(): lax.all_gather(local_factor, 'col', axis=0, tiled=True)  53.2 us
    all_gather x1, waiting for transfers between devices, shards(): col_factor = lax.all_gather(own_factor, 'row', axis=0, tiled=True)  33.7 us
    all_gather x1, blocking collectives, shards(): panel = lax.all_gather(panel_ids, 'col', axis=0, tiled=True)  20.6 us
    dot_general x8, matrix products, factor(): lax.dot_general(kernel[:, :finish], inverse[block_at * block_width:finish...  15.3 us
    dot_general x1, matrix products, shards(): lax.dot_general(lax.all_gather(local_factor, 'col', axis=0, tiled=True),...  12.5 us
    all_to_all x1, starting transfers between devices, shards(): lax.all_to_all(jnp.stack([rest_ids] * lax.axis_size(('row', 'col'))), ('r...  11.5 us
    gather x1, local copies, waits for them, and re-layouts, shards(): row_emb = teacher[row_ids]  11.3 us
    gather x1, local copies, waits for them, and re-layouts, shards(): panel_emb = teacher[panel]  11.1 us
  transfers between devices with their start and end apart: 3, of which 2 were waited for; matrix products, arithmetic and copies ran while one was open for 22% of the time, Pallas kernels for 0%

profile of v1, /device:TPU:1, one launch (start us, length us, event | category | flops | bytes accessed | tf_op | source)
XLA Modules:
  0.0 216.4 jit_solution(9260177902450704119)
XLA Ops:
  7.2 1.3 stack.2
  8.5 11.5 %all-to-all-start = ((s32[128,1,1,128]{3,2,1,0:T(1,128)}), s32[128,1,1,128]{3,2,1,0:T(1,128)S(1)}, u32[]{:S(2)}, u32[]{:S(2)}) async-start(s32[128,1,1,128]{3,2,1,0:T(1,128)} %stack.2), calls=%async_computation | async-start | bytes 131072 | tf_op jit(solution)/shard_map/all_to_all | solution.py:41
  20.0 20.6 %all-gather = s32[16,1,128]{2,1,0:T(1,128)S(1)} all-gather(s32[1,1,128]{2,1,0:T(1,128)} %bitcast.59), channel_id=1, replica_groups=mesh['row'=8,'col'=16] {'col'}, dimensions={0}, use_global_device_ids=true | all-gather | bytes 8704 | tf_op jit(solution)/shard_map/all_gather | solution.py:45
  40.6 11.1 %gather_fusion.3 = bf16[2048,256]{1,0:T(8,128)(2,1)S(1)} fusion(bf16[16384,256]{1,0:T(8,128)(2,1)} %param.4, s32[2048]{0:T(1024)S(1)} %fusion.49), kind=kCustom, calls=%fused_computation.3 | custom fusion | bytes 2105344 | tf_op jit(solution)/shard_map/gather | solution.py:46
  52.1 5.2 %gather_fusion.4 = bf16[128,256]{1,0:T(8,128)(2,1)S(1)} fusion(bf16[16384,256]{1,0:T(8,128)(2,1)} %param.4, s32[1024]{0:T(1024)S(1)} %get-tuple-element.8), kind=kCustom, calls=%fused_computation.4 | custom fusion | bytes 131584 | tf_op jit(solution)/shard_map/gather | solution.py:54
  58.0 1.3 convolution_convert_fusion
  59.3 1.7 convolution_convert_fusion.2
  61.1 2.4 %fusion.19 = bf16[128,512]{1,0:T(8,128)(2,1)S(1)} fusion(bf16[128,2048]{1,0:T(8,128)(2,1)S(1)} %fusion.7, bf16[2048,2048]{1,0:T(8,128)(2,1)} %param.7), kind=kOutput, calls=%fused_computation.27 | convolution fusion | flops 268500992 | bytes 2752512 | tf_op jit(solution)/shard_map/dot_general | solution.py:23
  63.5 2.1 fusion.25
  65.6 0.9 pad_maximum_fusion.1
  66.5 5.2 %gather_fusion.2 = bf16[128,256]{1,0:T(8,128)(2,1)S(1)} fusion(bf16[16384,256]{1,0:T(8,128)(2,1)} %param.4, s32[1024]{0:T(1024)S(1)} %get-tuple-element.9), kind=kCustom, calls=%fused_computation.2 | custom fusion | bytes 131584 | tf_op jit(solution)/shard_map/gather | solution.py:62
  72.4 1.4 convolution_convert_fusion.1
  73.7 1.8 convolution_convert_fusion.3
  75.5 2.2 %fusion.22 = bf16[128,512]{1,0:T(8,128)(2,1)S(1)} fusion(bf16[2048,2048]{1,0:T(8,128)(2,1)} %param.7, bf16[128,2048]{1,0:T(8,128)(2,1)S(1)} %fusion.6), kind=kOutput, calls=%fused_computation.32 | convolution fusion | flops 201392128 | bytes 2097152 | tf_op jit(solution)/shard_map/dot_general | solution.py:23
  77.7 2.4 %fusion.16 = bf16[128,512]{1,0:T(8,128)(2,1)S(1)} fusion(bf16[128,2048]{1,0:T(8,128)(2,1)S(1)} %fusion.6, bf16[2048,2048]{1,0:T(8,128)(2,1)} %param.7), kind=kOutput, calls=%fused_computation.26 | convolution fusion | flops 268500992 | bytes 2752512 | tf_op jit(solution)/shard_map/dot_general | solution.py:23
  80.1 0.8 pad_maximum_fusion
  81.1 11.3 %gather_fusion = bf16[2048,256]{1,0:T(8,128)(2,1)S(1)} fusion(bf16[16384,256]{1,0:T(8,128)(2,1)} %param.4, s32[2048]{0:T(1024)S(1)} %broadcast_clamp_fusion), kind=kCustom, calls=%fused_computation | custom fusion | bytes 2105344 | tf_op jit(solution)/shard_map/gather | solution.py:57
  92.4 7.9 %gather_fusion.1 = bf16[1024,256]{1,0:T(8,128)(2,1)S(1)} fusion(bf16[16384,256]{1,0:T(8,128)(2,1)} %param.4, s32[1024]{0:T(1024)S(1)} %broadcast_clamp_fusion.1), kind=kCustom, calls=%fused_computation.1 | custom fusion | bytes 1052672 | tf_op jit(solution)/shard_map/gather | solution.py:55
  100.9 0.8 pad_maximum_fusion.2
  101.8 33.7 %all-gather.6.cloned.1.call-done = bf16[1024,2048]{1,0:T(8,128)(2,1)} async-done(((bf16[128,2048]{1,0:T(8,128)(2,1)}), bf16[1024,2048]{1,0:T(8,128)(2,1)}) %all-gather.6.cloned.1.call-update) | async-done | bytes 4194320 | tf_op jit(solution)/shard_map/all_gather | solution.py:56
  135.5 53.2 %all-gather.4.cloned.1.call-done = bf16[2048,2048]{1,0:T(8,128)(2,1)} async-done(((bf16[128,2048]{1,0:T(8,128)(2,1)}), bf16[2048,2048]{1,0:T(8,128)(2,1)}) %all-gather.4.cloned.1.call-update) | async-done | bytes 8388624 | tf_op jit(solution)/shard_map/all_gather | solution.py:64
  188.7 12.5 %fusion.65 = f32[2048,1024]{1,0:T(8,128)S(1)} fusion(bf16[2048,2048]{1,0:T(8,128)(2,1)} %all-gather.4.cloned.1.call-done, bf16[1024,2048]{1,0:T(8,128)(2,1)} %all-gather.6.cloned.1.call-done), kind=kOutput, calls=%fused_computation.96 | convolution fusion | flops 8589934592 | bytes 20971520 | tf_op jit(solution)/shard_map/dot_general | solution.py:63
  201.3 2.7 %select_bitcast_fusion = f32[256,8,8,128]{3,1,2,0:T(8,128)S(1)} fusion(f32[2048,1024]{1,0:T(8,128)S(1)} %fusion.65, bf16[2048,256]{1,0:T(8,128)(2,1)S(1)} %gather_fusion, bf16[1024,256]{1,0:T(8,128)(2,1)S(1)} %gather_fusion.1, f32[1024]{0:T(1024)S(1)} %multiply_reduce_fusion.2, f32[2048]{0:T(1024)S(1)} %multiply_reduce_fusion.1, s32[1024]{0:T(1024)S(1)} %fusion.59, ...), kind=kOutput, calls=%fused_computation.5 | convolution fusion | flops 1088421888 | bytes 18374656 | tf_op jit(solution)/shard_map/dot_general | solution.py:10
  204.0 5.5 %copy.8 = f32[256,8,8,128]{3,2,1,0:T(8,128)} copy(f32[256,8,8,128]{3,1,2,0:T(8,128)S(1)} %select_bitcast_fusion) | data formatting | bytes 16777216
  (21 shorter events, 2.3 us)
Async XLA Ops:
  8.5 43.6 %all-to-all-start = ((s32[128,1,1,128]{3,2,1,0:T(1,128)}), s32[128,1,1,128]{3,2,1,0:T(1,128)S(1)}, u32[]{:S(2)}, u32[]{:S(2)}) async-start(s32[128,1,1,128]{3,2,1,0:T(1,128)} %stack.2), calls=%async_computation | async-start | bytes 131072 | tf_op jit(solution)/shard_map/all_to_all | solution.py:41
  20.0 115.5 %all-gather.6.cloned.1.call-start = ((), (), s32[]{:S(2)}) async-start(), calls=%async_computation.2 | async-start | bytes 4718592 | tf_op jit(solution)/shard_map/all_gather | solution.py:56
  66.5 122.3 %all-gather.4.cloned.1.call-start = ((), (), s32[]{:S(2)}) async-start(), calls=%async_computation.1 | async-start | bytes 8912896 | tf_op jit(solution)/shard_map/all_gather | solution.py:64
Sparse Core Ops, SparseCore 0:
  66.6 68.8 all-gather.5
  137.8 50.8 all-gather.3
